TPU v7x, 32 devices: a whole 2x2x4 slice. The times are simulated.
32 devices in a mesh: wide: 4 (over z), narrow: 8 (over y, x, core).
Axes of the slice: x: 2, y: 2, z: 4, core: 2. Of those that a mesh axis runs over, the one named last changes fastest.
Arguments:
- hidden_in: float32 [2, 32, 8192], P(None, None, 'narrow'), may hold values from -100 to 100
- attn_gain: float32 [8192], P('narrow'), may hold values from 0.1 to 1.9
- w_query: bfloat16 [8192, 8192], P('narrow', 'wide'), may hold values from -0.0625 to 0.0625
- w_key: bfloat16 [8192, 1024], P('narrow', 'wide'), may hold values from -0.0625 to 0.0625
- w_value: bfloat16 [8192, 1024], P('narrow', 'wide'), may hold values from -0.0625 to 0.0625
- w_out: bfloat16 [8192, 8192], P('wide', 'narrow'), may hold values from -0.0625 to 0.0625
- ffn_gain: float32 [8192], P('narrow'), may hold values from 0.1 to 1.9
- w_gate: bfloat16 [8192, 28672], P('narrow', 'wide'), may hold values from -0.0625 to 0.0625
- w_up: bfloat16 [8192, 28672], P('narrow', 'wide'), may hold values from -0.0625 to 0.0625
- w_down: bfloat16 [28672, 8192], P('wide', 'narrow'), may hold values from -0.03125 to 0.03125
- key_cache: bfloat16 [2, 32, 8, 2048, 128], P(None, 'narrow', 'wide'), may hold values from -256 to 256
- value_cache: bfloat16 [2, 32, 8, 2048, 128], P(None, 'narrow', 'wide'), may hold values from -6 to 6
- cache_len: int32 [2, 32], P(None, 'narrow'), may hold values from 1 to 2048, as said below
Outputs:
- hidden_out: float32 [2, 32, 8192], P(None, None, 'narrow')
Inputs may be any that keep to these rules, and one draw needn't show every extreme that they name: `cache_len`: in every micro-batch one row's cache holds exactly 2048 tokens.
All inputs are finite; a program needn't handle non-finite values.
Results may differ from a plain program's by a relative error of at most 0.0086.
Values may be sent and summed in bfloat16 or wider, within the bound.
A program may use at most 128 MiB of HBM per device.

v0:
```python
import jax
import jax.numpy as jnp
from jax import lax
from jax.sharding import PartitionSpec as P

D = 8192


epsilon = 1e-05


def rotate(values, places):
    halfway = values.shape[-1] // 2
    angles_base = 500000.0 ** (-jnp.arange(halfway, dtype=jnp.float32) * 2.0 / values.shape[-1])
    angles = places * angles_base
    cosines = jnp.cos(angles)
    sinewave = jnp.sin(angles)
    lower_half = values[..., :halfway]
    upper_half = values[..., halfway:]
    return jnp.concatenate(
        [
            lower_half * cosines - upper_half * sinewave,
            upper_half * cosines + lower_half * sinewave,
        ],
        axis=-1,
    )


def attend(queries, key_new, value_new, key_rows, value_rows, length):
    scaling = queries.shape[-1] ** (-0.5)
    scores = (
        jnp.einsum("kgd,kld->kgl", queries, key_rows, preferred_element_type=jnp.float32) * scaling
    )
    visible = jnp.arange(key_rows.shape[1]) < length
    scores = jnp.where(visible, scores, -jnp.inf)
    own_score = (
        jnp.einsum("kgd,kd->kg", queries, key_new, preferred_element_type=jnp.float32) * scaling
    )
    highest = jnp.maximum(jnp.max(scores, axis=-1), own_score)
    shifted = jnp.exp(scores - highest[..., None])
    own_term = jnp.exp(own_score - highest)
    totals = jnp.sum(shifted, axis=-1) + own_term
    weights = (shifted / totals[..., None]).astype(jnp.bfloat16)
    own_weight = (own_term / totals).astype(jnp.bfloat16)
    attended = jnp.einsum("kgl,kld->kgd", weights, value_rows, preferred_element_type=jnp.float32)
    attended = (
        attended
        + own_weight.astype(jnp.float32)[..., None] * value_new.astype(jnp.float32)[:, None, :]
    )
    return attended.astype(jnp.bfloat16)


def body(
    hidden_in,
    attn_gain,
    w_query,
    w_key,
    w_value,
    w_out,
    ffn_gain,
    w_gate,
    w_up,
    w_down,
    key_cache,
    value_cache,
    cache_len,
):
    head_size = key_cache.shape[-1]
    local_rows = key_cache.shape[1]
    kv_here = key_cache.shape[2]
    results = []
    for micro_index in range(hidden_in.shape[0]):
        stream = hidden_in[micro_index]
        squares = jnp.sum(stream * stream, axis=-1)
        normed = (stream * attn_gain).astype(jnp.bfloat16)
        query_part = jnp.dot(normed, w_query, preferred_element_type=jnp.float32)
        key_part = jnp.dot(normed, w_key, preferred_element_type=jnp.float32)
        value_part = jnp.dot(normed, w_value, preferred_element_type=jnp.float32)
        all_squares = lax.psum(squares, "narrow")
        query_rows, key_rows_new, value_rows_new = (
            lax.psum_scatter(query_part, "narrow", scatter_dimension=0, tiled=True),
            lax.psum_scatter(key_part, "narrow", scatter_dimension=0, tiled=True),
            lax.psum_scatter(value_part, "narrow", scatter_dimension=0, tiled=True),
        )
        own_squares = lax.dynamic_slice_in_dim(
            all_squares, lax.axis_index("narrow") * local_rows, local_rows
        )
        factor = lax.rsqrt(own_squares / D + epsilon)[:, None]
        places = cache_len[micro_index].astype(jnp.float32)[:, None, None]
        queries = rotate((query_rows * factor).reshape(local_rows, -1, head_size), places).astype(
            jnp.bfloat16
        )
        keys_new = rotate(
            (key_rows_new * factor).reshape(local_rows, kv_here, head_size), places
        ).astype(jnp.bfloat16)
        values_new = (
            (value_rows_new * factor).reshape(local_rows, kv_here, head_size).astype(jnp.bfloat16)
        )
        queries = queries.reshape(local_rows, kv_here, -1, head_size)
        attended = jax.vmap(attend)(
            queries,
            keys_new,
            values_new,
            key_cache[micro_index],
            value_cache[micro_index],
            cache_len[micro_index],
        )
        attended = attended.reshape(local_rows, -1)
        out_terms = jnp.dot(
            lax.all_gather(attended, "narrow", axis=0, tiled=True),
            w_out,
            preferred_element_type=jnp.float32,
        )
        middle = stream + lax.psum(out_terms, "wide")
        squares_two = jnp.sum(middle * middle, axis=-1)
        normed_two = (middle * ffn_gain).astype(jnp.bfloat16)
        gate_part = jnp.dot(normed_two, w_gate, preferred_element_type=jnp.float32)
        up_part = jnp.dot(normed_two, w_up, preferred_element_type=jnp.float32)
        gate_sum, up_sum, summed_two = lax.psum((gate_part, up_part, squares_two), "narrow")
        factor_two = lax.rsqrt(summed_two / D + epsilon)[:, None]
        hidden = (jax.nn.silu(gate_sum * factor_two) * (up_sum * factor_two)).astype(jnp.bfloat16)
        down_terms = jnp.dot(hidden, w_down, preferred_element_type=jnp.float32)
        results.append(middle + lax.psum(down_terms, "wide"))
    return jnp.stack(results)


def solution(mesh):
    return jax.shard_map(
        body,
        mesh=mesh,
        in_specs=(
            P(None, None, "narrow"),
            P("narrow"),
            P("narrow", "wide"),
            P("narrow", "wide"),
            P("narrow", "wide"),
            P("wide", "narrow"),
            P("narrow"),
            P("narrow", "wide"),
            P("narrow", "wide"),
            P("wide", "narrow"),
            P(None, "narrow", "wide", None, None),
            P(None, "narrow", "wide", None, None),
            P(None, "narrow"),
        ),
        out_specs=P(None, None, "narrow"),
        check_vma=False,
    )
```

profile of v0, /device:TPU:0, one launch (start us, length us, event | category | flops | bytes accessed | tf_op | source)
XLA Modules:
  0.0 363.3 jit_solution(15961159658953528360)
XLA Ops:
  9.1 1.8 fusion.89
  11.8 1.8 fusion.85
  13.7 3.7 %fusion.84 = f32[32,2048]{1,0:T(8,128)} fusion(bf16[32,1024]{1,0:T(8,128)(2,1)S(1)} %get-tuple-element.34, bf16[1024,2048]{1,0:T(8,128)(2,1)} %param.15), kind=kOutput, calls=%fused_computation.126 | convolution fusion | flops 134217728 | bytes 4521984 | tf_op jit(solution)/shard_map/dot_general | solution.py:76
  17.4 3.7 %fusion.88 = f32[32,2048]{1,0:T(8,128)} fusion(bf16[32,1024]{1,0:T(8,128)(2,1)S(1)} %get-tuple-element.33, bf16[1024,2048]{1,0:T(8,128)(2,1)} %param.15), kind=kOutput, calls=%fused_computation.130 | convolution fusion | flops 134217728 | bytes 4521984 | tf_op jit(solution)/shard_map/dot_general | solution.py:76
  22.6 46.5 %all-reduce.18.cloned.1.call-done = (f32[32]{0:T(128)}, f32[32,256]{1,0:T(8,128)}, f32[32,256]{1,0:T(8,128)}, f32[32]{0:T(128)}, f32[32,256]{1,0:T(8,128)}, /*index=5*/f32[32,256]{1,0:T(8,128)}) async-done(((f32[32]{0:T(128)}, f32[32,256]{1,0:T(8,128)}, f32[32,256]{1,0:T(8,128)}, f32[32]{0:T(128)}, f32[32,256]{1,0:T(8,128)}, /*index=5*/f32[32,256]{1,0:T(8,128)}), (f32[32]{0:T(128)}, f32[32,256]{1,0:T(8,128)}, ...) | async-done | bytes 131344 | tf_op jit(solution)/shard_map/psum | solution.py:79
  71.7 55.9 %all-reduce.22.cloned.1.call-done = (f32[32,2048]{1,0:T(8,128)}, f32[32,2048]{1,0:T(8,128)}) async-done(((f32[32,2048]{1,0:T(8,128)}, f32[32,2048]{1,0:T(8,128)}), (f32[32,2048]{1,0:T(8,128)}, f32[32,2048]{1,0:T(8,128)})) %all-reduce.22.cloned.1.call-update) | async-done | bytes 524304
  129.0 3.5 fusion.83
  132.8 2.9 fusion.33
  135.7 8.4 %all-gather = bf16[8,4,2048]{2,1,0:T(4,128)(2,1)S(1)} all-gather(bf16[1,4,2048]{2,1,0:T(4,128)(2,1)S(1)} %reshape.200), channel_id=1, replica_groups=mesh['wide'=4,'narrow'=8] {'narrow'}, dimensions={0}, use_global_device_ids=true | all-gather | bytes 147456 | tf_op jit(solution)/shard_map/all_gather | solution.py:110
  144.4 3.5 fusion.82
  148.2 2.9 fusion.30
  151.1 9.0 %all-gather.1 = bf16[8,4,2048]{2,1,0:T(4,128)(2,1)S(1)} all-gather(bf16[1,4,2048]{2,1,0:T(4,128)(2,1)S(1)} %reshape.202), channel_id=1, replica_groups=mesh['wide'=4,'narrow'=8] {'narrow'}, dimensions={0}, use_global_device_ids=true | all-gather | bytes 147456 | tf_op jit(solution)/shard_map/all_gather | solution.py:110
  160.2 3.7 %fusion.87 = f32[32,1024]{1,0:T(8,128)} fusion(bf16[32,2048]{1,0:T(8,128)(2,1)S(1)} %reshape.201, bf16[2048,1024]{1,0:T(8,128)(2,1)} %param.18), kind=kOutput, calls=%fused_computation.129 | convolution fusion | flops 134217728 | bytes 4456448 | tf_op jit(solution)/shard_map/dot_general | solution.py:109
  163.9 3.7 %fusion.91 = f32[32,1024]{1,0:T(8,128)} fusion(bf16[32,2048]{1,0:T(8,128)(2,1)S(1)} %reshape.203, bf16[2048,1024]{1,0:T(8,128)(2,1)} %param.18), kind=kOutput, calls=%fused_computation.133 | convolution fusion | flops 134217728 | bytes 4456448 | tf_op jit(solution)/shard_map/dot_general | solution.py:109
  167.8 35.4 %all-reduce.26.cloned.1.call-done = (f32[32,1024]{1,0:T(8,128)}, f32[32,1024]{1,0:T(8,128)}) async-done(((f32[32,1024]{1,0:T(8,128)}, f32[32,1024]{1,0:T(8,128)}), (f32[32,1024]{1,0:T(8,128)}, f32[32,1024]{1,0:T(8,128)})) %all-reduce.26.cloned.1.call-update) | async-done | bytes 262160 | tf_op jit(solution)/shard_map/psum | solution.py:114
  204.3 8.9 %fusion.54 = f32[32,7168]{1,0:T(8,128)} fusion(bf16[1024,7168]{1,0:T(8,128)(2,1)} %param.21, f32[32,1024]{1,0:T(8,128)S(1)} %get-tuple-element.26, f32[1024]{0:T(1024)S(1)} %copy-done.5), kind=kOutput, calls=%fused_computation.67 | convolution fusion | flops 469827584 | bytes 15732736 | tf_op jit(solution)/shard_map/dot_general | solution.py:118
  213.2 8.9 %fusion.55 = f32[32,7168]{1,0:T(8,128)} fusion(bf16[1024,7168]{1,0:T(8,128)(2,1)} %param.20, f32[32,1024]{1,0:T(8,128)S(1)} %get-tuple-element.26, f32[1024]{0:T(1024)S(1)} %copy-done.5), kind=kOutput, calls=%fused_computation.68 | convolution fusion | flops 469827584 | bytes 15732736 | tf_op jit(solution)/shard_map/dot_general | solution.py:117
  222.1 3.6 fusion.56
  225.7 3.6 fusion.57
  229.4 12.7 %all-reduce.6 = (f32[32]{0:T(128)S(1)}, f32[32]{0:T(128)S(1)}) all-reduce(f32[32]{0:T(128)S(1)} %get-tuple-element.31, f32[32]{0:T(128)S(1)} %get-tuple-element.25), channel_id=1, replica_groups=mesh['wide'=4,'narrow'=8] {'narrow'}, use_global_device_ids=true, to_apply=%region_23.24 | all-reduce | flops 64 | bytes 512 | tf_op jit(solution)/shard_map/psum | solution.py:119
  242.1 63.1 %all-reduce.20.cloned.1.call-done = (f32[32,7168]{1,0:T(8,128)}, f32[32,7168]{1,0:T(8,128)}, f32[32,7168]{1,0:T(8,128)}, f32[32,7168]{1,0:T(8,128)}) async-done(((f32[32,7168]{1,0:T(8,128)}, f32[32,7168]{1,0:T(8,128)}, f32[32,7168]{1,0:T(8,128)}, f32[32,7168]{1,0:T(8,128)}), (f32[32,7168]{1,0:T(8,128)}, f32[32,7168]{1,0:T(8,128)}, f32[32,7168]{1,0:T(8,128)}, ...) | async-done | bytes 3670032 | tf_op jit(solution)/shard_map/psum | solution.py:119
  305.2 9.2 %fusion.39 = f32[32,1024]{1,0:T(8,128)} fusion(bf16[7168,1024]{1,0:T(8,128)(2,1)} %param.22, f32[32,7168]{1,0:T(8,128)} %get-tuple-element.15, f32[32,7168]{1,0:T(8,128)} %get-tuple-element.16, f32[32]{0:T(128)S(1)} %add_rsqrt_fusion), kind=kOutput, calls=%fused_computation.29 | convolution fusion | flops 471597056 | bytes 16646272 | tf_op jit(solution)/shard_map/dot_general | solution.py:122
  315.0 3.4 fusion.38
  318.5 35.7 %all-reduce.24.cloned.1.call-done = (f32[32,1024]{1,0:T(8,128)}, f32[32,1024]{1,0:T(8,128)}) async-done(((f32[32,1024]{1,0:T(8,128)}, f32[32,1024]{1,0:T(8,128)}), (f32[32,1024]{1,0:T(8,128)}, f32[32,1024]{1,0:T(8,128)})) %all-reduce.24.cloned.1.call-update) | async-done | bytes 262160 | tf_op jit(solution)/shard_map/psum | solution.py:123
  (95 shorter events, 13.7 us)
Async XLA Ops:
  6.5 14.7 %copy-start.7 = (u32[32]{0:T(128)S(1)}, u32[32]{0:T(128)}, u32[]{:S(2)}) copy-start(u32[32]{0:T(128)} %constant.43) | copy-start | bytes 388
  6.5 14.7 %copy-start.6 = (s32[2,4]{1,0:T(2,128)S(1)}, s32[2,4]{1,0:T(2,128)}, u32[]{:S(2)}) copy-start(s32[2,4]{1,0:T(2,128)} %param.25) | copy-start | bytes 100
  6.5 62.5 %all-reduce.18.cloned.1.call-start = ((), (), s32[]{:S(2)}) async-start(), calls=%async_computation | async-start | bytes 264192 | tf_op jit(solution)/shard_map/psum | solution.py:79
  13.6 114.0 %all-reduce.22.cloned.1.call-start = ((), (), s32[]{:S(2)}) async-start(), calls=%async_computation.2 | async-start | bytes 1048576
  21.2 182.0 %all-reduce.26.cloned.1.call-start = ((), (), s32[]{:S(2)}) async-start(), calls=%async_computation.4 | async-start | bytes 524288 | tf_op jit(solution)/shard_map/psum | solution.py:114
  148.2 55.0 %copy-start.4 = (f32[2,32,1024]{2,1,0:T(8,128)S(1)}, f32[2,32,1024]{2,1,0:T(8,128)}, u32[]{:S(2)}) copy-start(f32[2,32,1024]{2,1,0:T(8,128)} %param.13) | copy-start | bytes 786436
  148.2 56.1 %copy-start.5 = (f32[1024]{0:T(1024)S(1)}, f32[1024]{0:T(1024)}, u32[]{:S(2)}) copy-start(f32[1024]{0:T(1024)} %param.19) | copy-start | bytes 12292
  167.6 137.6 %all-reduce.20.cloned.1.call-start = ((), (), s32[]{:S(2)}) async-start(), calls=%async_computation.1 | async-start | bytes 7340032 | tf_op jit(solution)/shard_map/psum | solution.py:119
  204.3 17.8 %slice-start.4 = ((s8[14680064]{0:T(1024)(128)(4,1)}), s8[4194304]{0:T(1024)(128)(4,1)S(1)}, s32[]{:S(2)}) async-start(s8[14680064]{0:T(1024)(128)(4,1)} %bitcast.117), calls=%async_computation.9 | async-start | bytes 8388608
  204.3 17.8 %slice-start.5 = ((s8[14680064]{0:T(1024)(128)(4,1)}), s8[4194304]{0:T(1024)(128)(4,1)S(1)}, s32[]{:S(2)}) async-start(s8[14680064]{0:T(1024)(128)(4,1)} %bitcast.117), calls=%async_computation.10 | async-start | bytes 8388608
  213.2 8.9 %slice-start.6 = ((s8[14680064]{0:T(1024)(128)(4,1)}), s8[4194304]{0:T(1024)(128)(4,1)S(1)}, s32[]{:S(2)}) async-start(s8[14680064]{0:T(1024)(128)(4,1)} %bitcast.117), calls=%async_computation.11 | async-start | bytes 8388608
  213.2 8.9 %slice-start.7 = ((s8[14680064]{0:T(1024)(128)(4,1)}), s8[2097152]{0:T(1024)(128)(4,1)S(1)}, s32[]{:S(2)}) async-start(s8[14680064]{0:T(1024)(128)(4,1)} %bitcast.117), calls=%async_computation.12 | async-start | bytes 4194304
  213.2 12.5 %slice-start.8 = ((s8[14680064]{0:T(1024)(128)(4,1)}), s8[4194304]{0:T(1024)(128)(4,1)S(1)}, s32[]{:S(2)}) async-start(s8[14680064]{0:T(1024)(128)(4,1)} %bitcast.119), calls=%async_computation.13 | async-start | bytes 8388608
  213.2 12.5 %slice-start.9 = ((s8[14680064]{0:T(1024)(128)(4,1)}), s8[4194304]{0:T(1024)(128)(4,1)S(1)}, s32[]{:S(2)}) async-start(s8[14680064]{0:T(1024)(128)(4,1)} %bitcast.119), calls=%async_computation.14 | async-start | bytes 8388608
  222.1 3.6 slice-start.10
  222.1 3.6 slice-start.11
  229.3 85.1 %slice-start = ((s8[14680064]{0:T(1024)(128)(4,1)}), s8[2097152]{0:T(1024)(128)(4,1)S(1)}, s32[]{:S(2)}) async-start(s8[14680064]{0:T(1024)(128)(4,1)} %bitcast.115), calls=%async_computation.5 | async-start | bytes 4194304
  229.3 124.9 %all-reduce.24.cloned.1.call-start = ((), (), s32[]{:S(2)}) async-start(), calls=%async_computation.3 | async-start | bytes 524288 | tf_op jit(solution)/shard_map/psum | solution.py:123
  305.2 9.3 %slice-start.1 = ((s8[14680064]{0:T(1024)(128)(4,1)}), s8[4194304]{0:T(1024)(128)(4,1)S(1)}, s32[]{:S(2)}) async-start(s8[14680064]{0:T(1024)(128)(4,1)} %bitcast.115), calls=%async_computation.6 | async-start | bytes 8388608
  305.2 9.3 %slice-start.2 = ((s8[14680064]{0:T(1024)(128)(4,1)}), s8[4194304]{0:T(1024)(128)(4,1)S(1)}, s32[]{:S(2)}) async-start(s8[14680064]{0:T(1024)(128)(4,1)} %bitcast.115), calls=%async_computation.7 | async-start | bytes 8388608
  305.2 9.4 %slice-start.3 = ((s8[14680064]{0:T(1024)(128)(4,1)}), s8[4194304]{0:T(1024)(128)(4,1)S(1)}, s32[]{:S(2)}) async-start(s8[14680064]{0:T(1024)(128)(4,1)} %bitcast.115), calls=%async_computation.8 | async-start | bytes 8388608
  305.2 9.6 %copy-start.2 = (f32[32,7168]{1,0:T(8,128)S(1)}, f32[32,7168]{1,0:T(8,128)}, u32[]{:S(2)}) copy-start(f32[32,7168]{1,0:T(8,128)} %get-tuple-element.17) | copy-start | bytes 2752516
  305.2 9.9 %copy-start.3 = (f32[32,7168]{1,0:T(8,128)S(1)}, f32[32,7168]{1,0:T(8,128)}, u32[]{:S(2)}) copy-start(f32[32,7168]{1,0:T(8,128)} %get-tuple-element.18) | copy-start | bytes 2752516
  314.4 42.4 %copy-start.1 = (bf16[1024,256]{1,0:T(8,128)(2,1)S(1)}, bf16[1024,256]{1,0:T(8,128)(2,1)}, u32[]{:S(2)}) copy-start(bf16[1024,256]{1,0:T(8,128)(2,1)} %param.17) | copy-start | bytes 1572868
  (1 other events, 1.8 us)
Sparse Core Ops, SparseCore 0:
  13.7 55.2 all-reduce.17
  72.2 55.4 all-reduce.21
  167.7 35.4 all-reduce.25
  229.4 75.6 all-reduce.19
  318.6 35.5 all-reduce.23
where the time goes:
time: 364 us; the launch traced here: 363 us
  waiting for transfers between devices  237 us (65%)
  matrix products  70.9 us (19%)
  blocking collectives  30.1 us (8%)
  between operations  14 us (4%)
  other arithmetic  9.9 us (3%)
    psum x1, waiting for transfers between devices, body(): lax.psum((gate_part, up_part, squares_two), 'narrow')  63.1 us
    unnamed x6, waiting for transfers between devices  56 us
    psum x1, waiting for transfers between devices, body(): all_squares = lax.psum(squares, 'narrow')  46.5 us
    psum x1, waiting for transfers between devices, body(): results.append(middle + lax.psum(down_terms, 'wide'))  35.7 us
    psum x1, waiting for transfers between devices, body(): middle = stream + lax.psum(out_terms, 'wide')  35.4 us
    all_gather x2, blocking collectives, body(): lax.all_gather(attended, 'narrow', axis=0, tiled=True)  17.4 us
    psum x1, blocking collectives, body(): lax.psum((gate_part, up_part, squares_two), 'narrow')  12.7 us
    dot_general x2, matrix products, body(): down_terms = jnp.dot(hidden, w_down, preferred_element_type=jnp.float32)  12.7 us
  transfers between devices with their start and end apart: 5, of which 5 were waited for; matrix products, arithmetic and copies ran while one was open for 3% of the time, Pallas kernels for 0%

commit v1 on v0

v1 whole, which is shorter than its diff:
```python
import functools

import jax
import jax.numpy as jnp
from jax import lax
from jax.experimental import pallas as pl
from jax.experimental.pallas import tpu as pltpu
from jax.sharding import PartitionSpec as P

D = 8192


epsilon = 1e-05
MESH = pl.DeviceIdType.MESH


def rotate(values, places):
    halfway = values.shape[-1] // 2
    angles_base = 500000.0 ** (-jnp.arange(halfway, dtype=jnp.float32) * 2.0 / values.shape[-1])
    angles = places * angles_base
    cosines = jnp.cos(angles)
    sinewave = jnp.sin(angles)
    lower_half = values[..., :halfway]
    upper_half = values[..., halfway:]
    return jnp.concatenate(
        [
            lower_half * cosines - upper_half * sinewave,
            upper_half * cosines + lower_half * sinewave,
        ],
        axis=-1,
    )


def attend(queries, key_new, value_new, key_rows, value_rows, length):
    scaling = queries.shape[-1] ** (-0.5)
    scores = (
        jnp.einsum("kgd,kld->kgl", queries, key_rows, preferred_element_type=jnp.float32) * scaling
    )
    visible = jnp.arange(key_rows.shape[1]) < length
    scores = jnp.where(visible, scores, -jnp.inf)
    own_score = (
        jnp.einsum("kgd,kd->kg", queries, key_new, preferred_element_type=jnp.float32) * scaling
    )
    highest = jnp.maximum(jnp.max(scores, axis=-1), own_score)
    shifted = jnp.exp(scores - highest[..., None])
    own_term = jnp.exp(own_score - highest)
    totals = jnp.sum(shifted, axis=-1) + own_term
    weights = (shifted / totals[..., None]).astype(jnp.bfloat16)
    own_weight = (own_term / totals).astype(jnp.bfloat16)
    attended = jnp.einsum("kgl,kld->kgd", weights, value_rows, preferred_element_type=jnp.float32)
    attended = (
        attended
        + own_weight.astype(jnp.float32)[..., None] * value_new.astype(jnp.float32)[:, None, :]
    )
    return attended.astype(jnp.bfloat16)


def enter(axis, n):
    barrier = pltpu.get_barrier_semaphore()
    me = lax.axis_index(axis)
    for step in range(1, n):
        pl.semaphore_signal(
            barrier, inc=1, device_id={axis: lax.rem(me + step, n)}, device_id_type=MESH
        )
    pl.semaphore_wait(barrier, n - 1)
    return me


def send_all(axis, n, source, target, send_sem, recv_sem):
    me = lax.axis_index(axis)
    copies = []
    for step in range(1, n):
        peer = lax.rem(me + step, n)
        copy = pltpu.make_async_remote_copy(
            src_ref=source(peer),
            dst_ref=target,
            send_sem=send_sem.at[step - 1],
            recv_sem=recv_sem.at[step - 1],
            device_id={axis: peer},
            device_id_type=MESH,
        )
        copy.start()
        copies.append(copy)
    return copies


def finish(copies):
    for copy in copies:
        copy.wait()


def total(arrived, n, columns):
    value = arrived[0, :, columns].astype(jnp.float32)
    for index in range(1, n):
        value = value + arrived[index, :, columns].astype(jnp.float32)
    return value


def sum_kernel(axis, n, blocks, out, arrived, send_sem, recv_sem):
    me = enter(axis, n)
    copies = send_all(axis, n, lambda peer: blocks.at[peer], arrived.at[me], send_sem, recv_sem)
    arrived[me] = blocks[me]
    finish(copies)
    out[...] = total(arrived, n, slice(None))


def spread_kernel(axis, n, block, out, send_sem, recv_sem):
    me = enter(axis, n)
    copies = send_all(axis, n, lambda peer: block, out.at[me], send_sem, recv_sem)
    out[me] = block[...]
    finish(copies)


def add_kernel(axis, n, blocks, stream, out, arrived, send_sem, recv_sem, send_two, recv_two):
    me = enter(axis, n)
    copies = send_all(axis, n, lambda peer: blocks.at[peer], arrived.at[me], send_sem, recv_sem)
    arrived[me] = blocks[me]
    finish(copies)
    out[me] = stream[me] + total(arrived, n, slice(None))
    finish(send_all(axis, n, lambda peer: out.at[me], out.at[me], send_two, recv_two))


def hidden_kernel(
    axis, n, blocks, out, arrived, mine, send_sem, recv_sem, send_two, recv_two
):
    me = enter(axis, n)
    copies = send_all(axis, n, lambda peer: blocks.at[peer], arrived.at[me], send_sem, recv_sem)
    arrived[me] = blocks[me]
    finish(copies)
    rows = blocks.shape[1] // 2
    width = blocks.shape[2] - 128
    half = width // 2
    squares = total(arrived, n, slice(width, width + 128))
    squares = squares[:rows, :1] + squares[rows:, :1]
    factor = lax.rsqrt(squares / D + epsilon)
    step = half // 7
    for start in range(0, half, step):
        parts = []
        for base in (0, half):
            sums = total(arrived, n, slice(base + start, base + start + step))
            gate = sums[:rows] * factor
            up = sums[rows:] * factor
            parts.append(gate / (1.0 + jnp.exp(-gate)) * up)
        mine[:, start : start + step] = jnp.concatenate(parts, axis=0).astype(jnp.bfloat16)
    copies = send_all(axis, n, lambda peer: mine, out.at[me], send_two, recv_two)
    out[me] = mine[...]
    finish(copies)


def call(kernel, axis, shape, dtype, scratch, phases, number, *operands):
    n = lax.axis_size(axis)
    whole = pl.BlockSpec(memory_space=pltpu.VMEM)
    return pl.pallas_call(
        functools.partial(kernel, axis, n),
        out_shape=jax.ShapeDtypeStruct(shape, dtype),
        in_specs=[whole] * len(operands),
        out_specs=whole,
        scratch_shapes=scratch + [pltpu.SemaphoreType.DMA((n - 1,))] * (2 * phases),
        compiler_params=pltpu.CompilerParams(
            collective_id=number, has_side_effects=True, vmem_limit_bytes=24 * 2**20
        ),
    )(*operands)


def sum_to_owner(blocks, axis, number):
    scratch = [pltpu.VMEM(blocks.shape, blocks.dtype)]
    return call(sum_kernel, axis, blocks.shape[1:], jnp.float32, scratch, 1, number, blocks)


def spread_matmul(halves, weights):
    owners, both, half = halves.shape
    left = halves[:, : both // 2].reshape(-1, half)
    right = halves[:, both // 2 :].reshape(-1, half)
    return jnp.dot(
        jnp.concatenate([left, right], axis=1), weights, preferred_element_type=jnp.float32
    )


def add_over_wide(stream, terms, number):
    n = lax.axis_size("wide")
    blocks = terms.reshape(n, terms.shape[0] // n, -1)
    return call(
        add_kernel,
        "wide",
        blocks.shape,
        jnp.float32,
        [pltpu.VMEM(blocks.shape, jnp.float32)],
        2,
        number,
        blocks,
        stream.reshape(blocks.shape),
    ).reshape(terms.shape)


def body(
    hidden_in,
    attn_gain,
    w_query,
    w_key,
    w_value,
    w_out,
    ffn_gain,
    w_gate,
    w_up,
    w_down,
    key_cache,
    value_cache,
    cache_len,
):
    head_size = key_cache.shape[-1]
    micro, local_rows, kv_here = key_cache.shape[:3]
    width = hidden_in.shape[2]
    narrow = lax.axis_size("narrow")
    own_rows = micro * local_rows
    rows = narrow * own_rows
    q_here = w_query.shape[1]
    k_here = w_key.shape[1]
    stream = hidden_in.reshape(micro, narrow, local_rows, width)
    stream = stream.transpose(1, 0, 2, 3).reshape(rows, width)
    squares = jnp.sum(stream * stream, axis=-1, keepdims=True)
    normed = (stream * attn_gain).astype(jnp.bfloat16)
    parts = jnp.concatenate(
        [
            jnp.dot(normed, w_query, preferred_element_type=jnp.float32),
            jnp.dot(normed, w_key, preferred_element_type=jnp.float32),
            jnp.dot(normed, w_value, preferred_element_type=jnp.float32),
            jnp.broadcast_to(squares, (rows, 128)),
        ],
        axis=1,
    )
    sums = sum_to_owner(parts.reshape(narrow, own_rows, -1), "narrow", 0)
    factor = lax.rsqrt(sums[:, -1:] / D + epsilon)
    places = cache_len.reshape(own_rows).astype(jnp.float32)[:, None, None]
    query_rows = sums[:, :q_here] * factor
    key_rows_new = sums[:, q_here : q_here + k_here] * factor
    value_rows_new = sums[:, q_here + k_here : q_here + 2 * k_here] * factor
    queries = rotate(query_rows.reshape(own_rows, -1, head_size), places).astype(jnp.bfloat16)
    keys_new = rotate(key_rows_new.reshape(own_rows, kv_here, head_size), places).astype(
        jnp.bfloat16
    )
    values_new = value_rows_new.reshape(own_rows, kv_here, head_size).astype(jnp.bfloat16)
    attended = jax.vmap(attend)(
        queries.reshape(own_rows, kv_here, -1, head_size),
        keys_new,
        values_new,
        key_cache.reshape((own_rows,) + key_cache.shape[2:]),
        value_cache.reshape((own_rows,) + value_cache.shape[2:]),
        cache_len.reshape(own_rows),
    ).reshape(own_rows, -1)
    half = attended.shape[1] // 2
    attended = jnp.concatenate([attended[:, :half], attended[:, half:]], axis=0)
    spread_shape = (narrow,) + attended.shape
    attended = call(
        spread_kernel, "narrow", spread_shape, jnp.bfloat16, [], 1, 1, attended
    )
    out_terms = spread_matmul(attended, w_out)
    middle = add_over_wide(stream, out_terms, 2)
    squares_two = jnp.sum(middle * middle, axis=-1, keepdims=True)
    coarse = lax.reduce_precision(squares_two, 8, 7)
    fine = squares_two - coarse
    normed_two = (middle * ffn_gain).astype(jnp.bfloat16)
    gate_part = jnp.dot(normed_two, w_gate, preferred_element_type=jnp.float32)
    up_part = jnp.dot(normed_two, w_up, preferred_element_type=jnp.float32)
    def beside(part, square):
        part = [part.astype(jnp.bfloat16), jnp.broadcast_to(square, (rows, 128)).astype(jnp.bfloat16)]
        return jnp.concatenate(part, axis=1).reshape(narrow, own_rows, -1)

    blocks = jnp.concatenate([beside(gate_part, coarse), beside(up_part, fine)], axis=1)
    hidden_shape = (narrow, 2 * own_rows, w_gate.shape[1] // 2)
    scratch = [pltpu.VMEM(blocks.shape, jnp.bfloat16), pltpu.VMEM(hidden_shape[1:], jnp.bfloat16)]
    hidden = call(hidden_kernel, "narrow", hidden_shape, jnp.bfloat16, scratch, 2, 3, blocks)
    down_terms = spread_matmul(hidden, w_down)
    result = add_over_wide(middle, down_terms, 4)
    result = result.reshape(narrow, micro, local_rows, width).transpose(1, 0, 2, 3)
    return result.reshape(hidden_in.shape)


def solution(mesh):
    return jax.shard_map(
        body,
        mesh=mesh,
        in_specs=(
            P(None, None, "narrow"),
            P("narrow"),
            P("narrow", "wide"),
            P("narrow", "wide"),
            P("narrow", "wide"),
            P("wide", "narrow"),
            P("narrow"),
            P("narrow", "wide"),
            P("narrow", "wide"),
            P("wide", "narrow"),
            P(None, "narrow", "wide", None, None),
            P(None, "narrow", "wide", None, None),
            P(None, "narrow"),
        ),
        out_specs=P(None, None, "narrow"),
        check_vma=False,
    )
```

time: 364 us -> 121 us (0.33)
  waiting for transfers between devices: 237 us -> 0 us
  Pallas kernels: 0 us -> 86.2 us
  matrix products: 70.9 us -> 28.4 us
  blocking collectives: 30.1 us -> 0 us
  between operations: 14 us -> 0.43 us
  other arithmetic: 9.9 us -> 2.43 us
    psum x4 -> x0, waiting for transfers between devices: 181 us -> none  [the longest x1 63.1 us: body(): lax.psum((gate_part, up_part, squares_two), 'narrow')]
    pallas_call x0 -> x5, Pallas kernels: none -> 86.2 us  [call(): pl.pallas_call(functools.partial(kernel, axis, n), out_shape=jax.ShapeDty...]
    unnamed x6 -> x0, waiting for transfers between devices: 56 us -> none
    dot_general x10 -> x5, matrix products: 32.8 us -> 8.74 us  [the longest x1 3.62 us: body(): jnp.dot(normed, w_query, preferred_element_type=jnp.float32)]
    all_gather x2 -> x0, blocking collectives: 17.4 us -> none  [body(): lax.all_gather(attended, 'narrow', axis=0, tiled=True)]
    psum x1 -> x0, blocking collectives: 12.7 us -> none  [body(): lax.psum((gate_part, up_part, squares_two), 'narrow')]
    dot_general x2 -> x1, matrix products: 12.5 us -> 7.83 us  [body(): up_part = jnp.dot(normed_two, w_up, preferred_element_type=jnp.float32)]
    dot_general x2 -> x1, matrix products: 7 us -> 2.4 us  [attend(): jnp.einsum('kgd,kld->kgl', queries, key_rows, preferred_element_type=jnp....]
  transfers between devices with their start and end apart: 5 -> 0, of which waited for: 5 -> 0; matrix products, arithmetic and copies ran while one was open for 3% -> 0% of each run, Pallas kernels for 0% -> 0%
where the time goes in v1:
time: 121 us
  Pallas kernels  86.2 us (71%)
  matrix products  28.4 us (23%)
  local copies, waits for them, and re-layouts  3.52 us (3%)
  other arithmetic  2.43 us (2%)
    pallas_call x5, Pallas kernels, call(): pl.pallas_call(functools.partial(kernel, axis, n), out_shape=jax.ShapeDty...  86.2 us
    dot_general x1, matrix products, body(): gate_part = jnp.dot(normed_two, w_gate, preferred_element_type=jnp.float32)  7.98 us
    dot_general x1, matrix products, body(): up_part = jnp.dot(normed_two, w_up, preferred_element_type=jnp.float32)  7.83 us
    dot_general x1, matrix products, body(): jnp.dot(normed, w_query, preferred_element_type=jnp.float32)  3.62 us
    dot_general x2, matrix products, spread_matmul(): jnp.dot(jnp.concatenate([left, right], axis=1), weights, preferred_elemen...  3.51 us

profile of v1, /device:TPU:0, one launch (start us, length us, event | category | flops | bytes accessed | tf_op | source)
XLA Modules:
  0.0 121.0 jit_solution(8617276750497093093)
XLA Ops:
  0.0 0.8 lt.16
  0.8 0.1 multiply_cosine_fusion
  1.0 1.0 reshape.165
  2.1 0.1 multiply_reduce_fusion.1
  2.6 0.7 multiply_convert_fusion
  3.3 0.2 fusion.30
  3.6 1.4 %fusion.29 = f32[64,256]{1,0:T(8,128)S(1)} fusion(bf16[64,1024]{1,0:T(8,128)(2,1)S(1)} %multiply_convert_fusion, bf16[1024,256]{1,0:T(8,128)(2,1)} %param.16), kind=kOutput, calls=%fused_computation.71 | convolution fusion | flops 33554432 | bytes 720896 | tf_op jit(solution)/shard_map/dot_general | solution.py:225
  5.0 3.6 %fusion.28 = f32[64,2048]{1,0:T(8,128)S(1)} fusion(bf16[64,1024]{1,0:T(8,128)(2,1)S(1)} %multiply_convert_fusion, bf16[1024,2048]{1,0:T(8,128)(2,1)} %param.15), kind=kOutput, calls=%fused_computation.70 | convolution fusion | flops 268435456 | bytes 4849664 | tf_op jit(solution)/shard_map/dot_general | solution.py:224
  8.7 12.0 %shard_map.127 = f32[8,2688]{1,0:T(8,128)S(1)} custom-call(f32[8,8,2688]{2,1,0:T(8,128)S(1)} %maximum_bitcast_fusion.2.blocks), custom_call_target="tpu_custom_call" | custom-call | tf_op jit(solution)/shard_map/pallas_call | solution.py:153
  20.7 0.2 rsqrt_reduce_fusion
  21.3 0.2 fusion.15
  21.5 2.4 %fusion.27 = (f32[8,2,8]{2,1,0:T(2,128)S(1)}, f32[8,2,8,2048]{3,2,1,0:T(8,128)S(1)}) fusion(bf16[8,2,2048,128]{3,2,1,0:T(8,128)(2,1)S(1)} %bitcast.72, bf16[8,2,8,64]{3,2,1,0:T(8,128)(2,1)S(1)} %get-tuple-element.25, bf16[8,2,8,64]{3,2,1,0:T(8,128)(2,1)S(1)} %get-tuple-element.26, pred[8,2048]{1,0:T(8,128)(4,1)S(1)} %iota_compare_fusion), kind=kOutput, calls=%fused_computation.69 | convolution fusion | flops 67960704 | bytes 9486848 | tf_op jit(solution)/shard_map/vmap(kgd,kld->kgl)/dot_general | solution.py:37
  23.9 0.3 fusion.3
  24.3 1.3 %fusion.2 = bf16[1,8,16,128]{3,2,1,0:T(8,128)(2,1)S(1)} fusion(bf16[8,2,2048,128]{3,2,1,0:T(8,128)(2,1)S(1)} %bitcast.71, f32[8,2,8,2048]{3,2,1,0:T(8,128)S(1)} %get-tuple-element.24, f32[8,2,8]{2,1,0:T(2,128)S(1)} %get-tuple-element.16, f32[8,2,8]{2,1,0:T(2,128)S(1)} %multiply_maximum_fusion, f32[8,2,128]{2,1,0:T(2,128)S(1)} %copy.22, ...), kind=kOutput, calls=%fused_computation.7 | convolution fusion | flops 67944448 | bytes 9479680 | tf_op jit(solution)/shard_map/vmap(kgl,kld->kgd)/dot_general | solution.py:50
  25.6 7.0 %shard_map.128 = bf16[8,16,1024]{2,1,0:T(8,128)(2,1)S(1)} custom-call(bf16[16,1024]{1,0:T(8,128)(2,1)S(1)} %pad_maximum_fusion.2.block), custom_call_target="tpu_custom_call" | custom-call | tf_op jit(solution)/shard_map/pallas_call | solution.py:153
  32.7 0.9 fusion.10
  33.6 15.5 %shard_map.129.stream = f32[4,16,1024]{2,1,0:T(8,128)S(1)} custom-call(f32[4,16,1024]{2,1,0:T(8,128)S(1)} %bitcast.66, f32[4,16,1024]{2,1,0:T(8,128)S(1)} %reshape_reshape.6.stream), custom_call_target="tpu_custom_call" | custom-call | tf_op jit(solution)/shard_map/pallas_call | solution.py:153
  49.5 7.8 %convolution_convert_fusion = bf16[64,7168]{1,0:T(8,128)(2,1)S(1)} fusion(bf16[64,1024]{1,0:T(8,128)(2,1)S(1)} %fusion.14, bf16[1024,7168]{1,0:T(8,128)(2,1)} %param.21), kind=kOutput, calls=%fused_computation | convolution fusion | flops 939982848 | bytes 15728640 | tf_op jit(solution)/shard_map/dot_general | solution.py:263
  57.4 8.0 %convolution_convert_fusion.1 = bf16[64,7168]{1,0:T(8,128)(2,1)S(1)} fusion(bf16[64,1024]{1,0:T(8,128)(2,1)S(1)} %fusion.14, bf16[1024,7168]{1,0:T(8,128)(2,1)} %param.20), kind=kOutput, calls=%fused_computation.1 | convolution fusion | flops 939982848 | bytes 15728640 | tf_op jit(solution)/shard_map/dot_general | solution.py:262
  65.5 0.1 pad_maximum_fusion.blocks
  65.6 34.0 %shard_map.130 = bf16[8,16,3584]{2,1,0:T(8,128)(2,1)S(1)} custom-call(bf16[8,16,7296]{2,1,0:T(8,128)(2,1)S(1)} %pad_maximum_fusion.blocks), custom_call_target="tpu_custom_call" | custom-call | tf_op jit(solution)/shard_map/pallas_call | solution.py:153
  99.7 2.7 %fusion.4 = f32[64,1024]{1,0:T(8,128)S(1)} fusion(bf16[7168,1024]{1,0:T(8,128)(2,1)S(1)} %bitcast.68, bf16[64,3584]{1,0:T(8,128)(2,1)S(1)} %get-tuple-element.6, bf16[64,3584]{1,0:T(8,128)(2,1)S(1)} %get-tuple-element.5), kind=kOutput, calls=%fused_computation.13 | convolution fusion | flops 941359104 | bytes 15859712 | tf_op jit(solution)/shard_map/dot_general | solution.py:174
  102.4 17.7 %shard_map.131 = f32[4,16,1024]{2,1,0:T(8,128)S(1)} custom-call(f32[4,16,1024]{2,1,0:T(8,128)S(1)} %bitcast.65, f32[4,16,1024]{2,1,0:T(8,128)S(1)} %shard_map.129.stream), custom_call_target="tpu_custom_call" | custom-call | tf_op jit(solution)/shard_map/pallas_call | solution.py:153
  120.2 0.8 reshape.182
  (57 shorter events, 1.7 us)
Async XLA Ops:
  0.0 3.3 %copy-start = (bf16[1024,256]{1,0:T(8,128)(2,1)S(1)}, bf16[1024,256]{1,0:T(8,128)(2,1)}, u32[]{:S(2)}) copy-start(bf16[1024,256]{1,0:T(8,128)(2,1)} %param.17) | copy-start | bytes 1572868
  3.5 18.0 %copy-start.2 = (bf16[2,4,2,2048,128]{4,3,2,1,0:T(8,128)(2,1)S(1)}, bf16[2,4,2,2048,128]{4,3,2,1,0:T(8,128)(2,1)}, u32[]{:S(2)}) copy-start(bf16[2,4,2,2048,128]{4,3,2,1,0:T(8,128)(2,1)} %param.23) | copy-start | bytes 25165828
  5.0 19.3 %slice-start.4 = ((s8[8388608]{0:T(1024)(128)(4,1)}), s8[4194304]{0:T(1024)(128)(4,1)S(1)}, s32[]{:S(2)}) async-start(s8[8388608]{0:T(1024)(128)(4,1)} %bitcast.69), calls=%async_computation.4 | async-start | bytes 8388608
  21.5 2.8 %slice-start.5 = ((s8[8388608]{0:T(1024)(128)(4,1)}), s8[4194304]{0:T(1024)(128)(4,1)S(1)}, s32[]{:S(2)}) async-start(s8[8388608]{0:T(1024)(128)(4,1)} %bitcast.69), calls=%async_computation.5 | async-start | bytes 8388608
  24.3 8.4 %copy-start.3 = (bf16[2048,1024]{1,0:T(8,128)(2,1)S(1)}, bf16[2048,1024]{1,0:T(8,128)(2,1)}, u32[]{:S(2)}) copy-start(bf16[2048,1024]{1,0:T(8,128)(2,1)} %param.18) | copy-start | bytes 12582916
  25.6 23.8 %copy-start.4 = (f32[1024]{0:T(1024)S(1)}, f32[1024]{0:T(1024)}, u32[]{:S(2)}) copy-start(f32[1024]{0:T(1024)} %param.19) | copy-start | bytes 12292
  57.4 42.3 %slice-start = ((s8[14680064]{0:T(1024)(128)(4,1)}), s8[4194304]{0:T(1024)(128)(4,1)S(1)}, s32[]{:S(2)}) async-start(s8[14680064]{0:T(1024)(128)(4,1)} %bitcast.67), calls=%async_computation | async-start | bytes 8388608
  57.4 42.3 %slice-start.1 = ((s8[14680064]{0:T(1024)(128)(4,1)}), s8[4194304]{0:T(1024)(128)(4,1)S(1)}, s32[]{:S(2)}) async-start(s8[14680064]{0:T(1024)(128)(4,1)} %bitcast.67), calls=%async_computation.1 | async-start | bytes 8388608
  57.4 42.3 %slice-start.2 = ((s8[14680064]{0:T(1024)(128)(4,1)}), s8[4194304]{0:T(1024)(128)(4,1)S(1)}, s32[]{:S(2)}) async-start(s8[14680064]{0:T(1024)(128)(4,1)} %bitcast.67), calls=%async_computation.2 | async-start | bytes 8388608
  65.5 34.2 %slice-start.3 = ((s8[14680064]{0:T(1024)(128)(4,1)}), s8[2097152]{0:T(1024)(128)(4,1)S(1)}, s32[]{:S(2)}) async-start(s8[14680064]{0:T(1024)(128)(4,1)} %bitcast.67), calls=%async_computation.3 | async-start | bytes 4194304
  99.7 21.3 %copy-start.1 = (bf16[1024,256]{1,0:T(8,128)(2,1)S(1)}, bf16[1024,256]{1,0:T(8,128)(2,1)}, u32[]{:S(2)}) copy-start(bf16[1024,256]{1,0:T(8,128)(2,1)} %param.17) | copy-start | bytes 1572868
